TPU v7x, 32 devices: a whole 2x2x4 slice. The times are simulated.
32 devices in a mesh: row: 4 (over y, core), col: 8 (over z, x).
Axes of the slice: x: 2, y: 2, z: 4, core: 2. Of those that a mesh axis runs over, the one named last changes fastest.
Arguments:
- transition: bfloat16 [32768, 32768], P('row', 'col'), may hold values from 1.5258789e-06 to 0.0024414062, as said below
- emission: bfloat16 [96, 32768], P(None, 'col'), may hold values from 0.0099487305 to 1
- token_ids: int32 [2, 192], replicated, may hold values from 0 to 95
- forward: bfloat16 [2, 192, 32768], P(None, 'col', 'row'), may hold values from 3.0517578e-06 to 0.0008239746, as said below
- backward_last: float32 [192, 32768], P('row', 'col'), may hold values from 0.1 to 10
Outputs:
- backward: float32 [2, 192, 32768], P(None, 'col', 'row')
- counts: float32 [32768, 1024], P('row', 'col')
Inputs may be any that keep to these rules, and one draw needn't show every extreme that they name: Positive transition weights. Positive forward weights.
All inputs are finite; a program needn't handle non-finite values.
Results may differ from a plain program's by a relative error of at most 0.00048.
Values may be sent and summed in bfloat16 or wider, within the bound.
A program may use at most 192 MiB of HBM per device.

v0:
```python
import jax
import jax.numpy as jnp
from jax import lax
from jax.sharding import PartitionSpec as P

H = 32768
N = 192
DW = 128
CHUNKS = 2


def reduce_scatter(partial, scale, col_count, col_index, local_seqs):
    half = col_count // 2
    width = partial.shape[1]
    scaled = (partial * scale).reshape(half, 2, local_seqs, width)
    side = col_index % 2
    away = lax.dynamic_index_in_dim(scaled, 1 - side, 1, keepdims=False).astype(jnp.float16)
    got = lax.ppermute(away, "col", [(c, c ^ 1) for c in range(col_count)])
    pair = lax.dynamic_index_in_dim(scaled, side, 1, keepdims=False) + got.astype(jnp.float32)
    here = col_index // 2
    total = lax.dynamic_index_in_dim(pair, here, 0, keepdims=False)
    packed = pair.astype(jnp.float16)
    for k in range(1, half):
        piece = lax.dynamic_index_in_dim(packed, (here + k) % half, 0, keepdims=False)
        got = lax.ppermute(piece, "col", [(c, (c + 2 * k) % col_count) for c in range(col_count)])
        total = total + got.astype(jnp.float32)
    return total


def on_device(transition, emission, token_ids, forward, backward_last):
    row_count = lax.axis_size("row")
    col_count = lax.axis_size("col")
    row_index = lax.axis_index("row")
    col_index = lax.axis_index("col")
    ratio = col_count // row_count
    local_seqs = forward.shape[1]
    row_seqs = backward_last.shape[0]
    block_src = transition.shape[0]
    block_dst = transition.shape[1]
    seq_total = local_seqs * col_count
    forward_all = [None, lax.all_gather(forward[1], "col", axis=0, tiled=True)]
    columns = lax.broadcasted_iota(jnp.int32, (row_seqs, emission.shape[0]), 1)
    window = transition[:, :DW]
    totals = jnp.zeros((block_src, DW), jnp.float32)
    outputs = [None, None]
    beta = backward_last
    scale = jnp.full((seq_total, 1), 64.0, jnp.float32)
    chunk = block_src // CHUNKS
    for step in (1, 0):
        tokens = lax.dynamic_slice_in_dim(token_ids[step], row_index * row_seqs, row_seqs, 0)
        onehot = (tokens[:, None] == columns).astype(jnp.bfloat16)
        emitted = jnp.dot(onehot, emission, preferred_element_type=jnp.float32)
        local_back = (emitted * beta).astype(jnp.bfloat16)
        weighted_back = lax.all_gather(local_back, "row", axis=0, tiled=True)
        pieces = []
        norm = jnp.zeros((seq_total,), jnp.float32)
        mass = jnp.zeros((seq_total,), jnp.float32)
        if step == 0:
            forward_all[0] = lax.all_gather(forward[0], "col", axis=0, tiled=True)
        for k in range(CHUNKS):
            rows = slice(k * chunk, (k + 1) * chunk)
            partial = lax.dot_general(
                weighted_back,
                transition[rows],
                (((1,), (1,)), ((), ())),
                preferred_element_type=jnp.float32,
            )
            norm = norm + jnp.sum(forward_all[step][:, rows].astype(jnp.float32) * partial, axis=1)
            mass = mass + jnp.sum(partial, axis=1)
            pieces.append(reduce_scatter(partial, scale, col_count, col_index, local_seqs))
        if step == 1:
            both = lax.psum(jnp.stack([norm, mass]), ("row", "col"))
            normal_all = both[0]
        else:
            normal_all = lax.psum(norm, ("row", "col"))
        normal_mine = lax.dynamic_slice_in_dim(normal_all, col_index * local_seqs, local_seqs, 0)
        scale_mine = lax.dynamic_slice_in_dim(scale, col_index * local_seqs, local_seqs, 0)
        mine = jnp.concatenate(pieces, axis=1) / (scale_mine * normal_mine[:, None])
        outputs[step] = mine
        if step == 1:
            halves = mine.reshape(local_seqs, ratio, block_dst)
            arrived = []
            for p in range(ratio):
                part = lax.dynamic_index_in_dim(halves, (col_index + p) % ratio, 1, keepdims=False)
                moves = []
                for r in range(row_count):
                    for c in range(col_count):
                        h = (c + p) % ratio
                        moves.append((r * col_count + c, c // ratio * col_count + r * ratio + h))
                arrived.append(lax.ppermute(part, ("row", "col"), moves))
            turned = jnp.stack([arrived[-i % ratio] for i in range(ratio)] * 2)
            start = (ratio - col_index % ratio) % ratio
            beta = lax.dynamic_slice_in_dim(turned, start, ratio, 0).reshape(row_seqs, block_dst)
            scale = (16777216.0 * both[0] / both[1])[:, None]
        scaled = (forward_all[step].astype(jnp.float32) / normal_all[:, None]).astype(jnp.bfloat16)
        totals = totals + lax.dot_general(
            scaled,
            weighted_back[:, :DW],
            (((0,), (0,)), ((), ())),
            preferred_element_type=jnp.float32,
        )
    counts = window.astype(jnp.float32) * totals * (H * H / N)
    return (jnp.stack(outputs), counts)


def solution(mesh):
    in_specs = (P("row", "col"), P(None, "col"), P(), P(None, "col", "row"), P("row", "col"))
    out_specs = (P(None, "col", "row"), P("row", "col"))
    return jax.shard_map(
        on_device, mesh=mesh, in_specs=in_specs, out_specs=out_specs, check_vma=False
    )
```

profile of v0, /device:TPU:0, one launch (start us, length us, event | category | flops | bytes accessed | tf_op | source)
XLA Modules:
  0.0 469.5 jit_solution(5049262565942433598)
XLA Ops:
  7.2 0.8 fusion.52
  8.1 0.3 copy-done
  8.3 2.2 fusion.10
  10.6 2.0 fusion.50
  12.8 20.2 %all-gather.7.cloned.1.call-done = bf16[192,4096]{1,0:T(8,128)(2,1)} async-done(((bf16[48,4096]{1,0:T(8,128)(2,1)}), bf16[192,4096]{1,0:T(8,128)(2,1)}) %all-gather.7.cloned.1.call-update) | async-done | bytes 1572880 | tf_op jit(solution)/shard_map/all_gather | solution.py:54
  33.1 21.2 %fusion.6 = f32[192,4096]{1,0:T(8,128)} fusion(bf16[192,4096]{1,0:T(8,128)(2,1)} %all-gather.7.cloned.1.call-done, bf16[8192,4096]{1,0:T(8,128)(2,1)} %param.5), kind=kOutput, calls=%fused_computation.6 | convolution fusion | flops 6442450944 | bytes 38273024 | tf_op jit(solution)/shard_map/dot_general | solution.py:62
  54.3 42.0 %all-gather.11.cloned.1.call-done = bf16[1,192,8192]{2,1,0:T(8,128)(2,1)} async-done(((bf16[1,24,8192]{2,1,0:T(8,128)(2,1)}), bf16[1,192,8192]{2,1,0:T(8,128)(2,1)}) %all-gather.11.cloned.1.call-update) | async-done | bytes 3145744 | tf_op jit(solution)/shard_map/all_gather | solution.py:41
  96.3 20.1 %multiply_reduce_fusion.2 = (f32[192]{0:T(256)S(1)}, f32[192]{0:T(256)S(1)}, f32[192]{0:T(256)S(1)}, f32[192]{0:T(256)S(1)}, f32[192,4096]{1,0:T(8,128)}, /*index=5*/f32[192,4096]{1,0:T(8,128)}) fusion(bf16[192,8192]{1,0:T(8,128)(2,1)} %bitcast.147, f32[192,4096]{1,0:T(8,128)} %fusion.6, bf16[192,4096]{1,0:T(8,128)(2,1)S(1)} %copy-done.6, ...), kind=kOutput, calls=%fused_computation.18 | convolution fusion | flops 6450315264 | bytes 47713280 | tf_op jit(solution)/shard_map/dot_general | solution.py:62
  116.4 2.4 fusion.14
  118.8 0.6 collective-permute-start.4
  119.4 1.5 fusion.13
  120.9 1.5 collective-permute-start
  122.4 65.4 %psum.14 = f32[2,192]{1,0:T(2,128)S(1)} all-reduce(f32[2,192]{1,0:T(2,128)S(1)} %pad_maximum_fusion.1), channel_id=1, replica_groups=mesh['row'=4,'col'=8] {'row','col'}, use_global_device_ids=true, to_apply=%region_4.5 | all-reduce | flops 384 | bytes 3072 | tf_op jit(solution)/shard_map/psum | solution.py:72
  188.0 1.8 fusion.49
  189.9 0.9 collective-permute-start.5
  190.8 2.9 collective-permute-start.7
  193.8 0.3 fusion.48
  194.2 0.6 collective-permute-start.1
  194.8 3.3 collective-permute-start.3
  198.0 1.5 collective-permute-done.5
  199.6 6.6 %collective-permute-start.2 = (f16[24,4096]{1,0:T(8,128)(2,1)S(1)}, f16[24,4096]{1,0:T(8,128)(2,1)S(1)}, u32[]{:S(2)}, u32[]{:S(2)}) collective-permute-start(f16[24,4096]{1,0:T(8,128)(2,1)S(1)} %get-tuple-element.36), channel_id=1, source_target_pairs={{0,4},{1,5},{2,6},{3,7},{4,0},{5,1},{6,2},{7,3},{8,12},{9,13},{10,... | collective-permute-start | bytes 589832 | tf_op jit(solution)/shard_map/ppermute | solution.py:25
  206.2 12.6 %collective-permute-done.6 = f16[24,4096]{1,0:T(8,128)(2,1)S(1)} collective-permute-done((f16[24,4096]{1,0:T(8,128)(2,1)S(1)}, f16[24,4096]{1,0:T(8,128)(2,1)S(1)}, u32[]{:S(2)}, u32[]{:S(2)}) %collective-permute-start.6) | collective-permute-done | bytes 196640 | tf_op jit(solution)/shard_map/ppermute | solution.py:25
  218.9 7.1 %collective-permute-done.2 = f16[24,4096]{1,0:T(8,128)(2,1)S(1)} collective-permute-done((f16[24,4096]{1,0:T(8,128)(2,1)S(1)}, f16[24,4096]{1,0:T(8,128)(2,1)S(1)}, u32[]{:S(2)}, u32[]{:S(2)}) %collective-permute-start.2) | collective-permute-done | bytes 196640 | tf_op jit(solution)/shard_map/ppermute | solution.py:25
  226.2 1.4 collective-permute-start.9
  227.7 0.7 collective-permute-start.8
  228.5 13.4 %collective-permute-done.9 = f32[24,4096]{1,0:T(8,128)S(1)} collective-permute-done((f32[24,4096]{1,0:T(8,128)S(1)}, f32[24,4096]{1,0:T(8,128)S(1)}, u32[]{:S(2)}, u32[]{:S(2)}) %collective-permute-start.9) | collective-permute-done | bytes 393248 | tf_op jit(solution)/shard_map/ppermute | solution.py:90
  242.0 1.1 fusion.20
  243.4 0.3 all-gather.13.cloned.1.call-update
  243.7 5.4 %fusion.12 = f32[8192,128]{1,0:T(8,128)} fusion(f32[192]{0:T(256)S(1)} %bitcast.143, bf16[192,4096]{1,0:T(8,128)(2,1)} %all-gather.7.cloned.1.call-done, bf16[1,192,8192]{2,1,0:T(8,128)(2,1)} %all-gather.11.cloned.1.call-done), kind=kOutput, calls=%fused_computation.20 | convolution fusion | flops 407371776 | bytes 7389952 | tf_op jit(solution)/shard_map/dot_general | solution.py:96
  249.3 32.2 %all-gather.9.cloned.1.call-done = bf16[192,4096]{1,0:T(8,128)(2,1)} async-done(((bf16[48,4096]{1,0:T(8,128)(2,1)}), bf16[192,4096]{1,0:T(8,128)(2,1)}) %all-gather.9.cloned.1.call-update) | async-done | bytes 1572880 | tf_op jit(solution)/shard_map/all_gather | solution.py:54
  281.4 21.3 %fusion.4 = f32[192,4096]{1,0:T(8,128)} fusion(bf16[192,4096]{1,0:T(8,128)(2,1)} %all-gather.9.cloned.1.call-done, bf16[8192,4096]{1,0:T(8,128)(2,1)} %param.5), kind=kOutput, calls=%fused_computation.4 | convolution fusion | flops 6442450944 | bytes 38273024 | tf_op jit(solution)/shard_map/dot_general | solution.py:62
  302.8 41.2 %all-gather.13.cloned.1.call-done = bf16[1,192,8192]{2,1,0:T(8,128)(2,1)} async-done(((bf16[1,24,8192]{2,1,0:T(8,128)(2,1)}), bf16[1,192,8192]{2,1,0:T(8,128)(2,1)}) %all-gather.13.cloned.1.call-update) | async-done | bytes 3145744 | tf_op jit(solution)/shard_map/all_gather | solution.py:59
  344.0 20.1 %multiply_reduce_fusion = (f32[192]{0:T(256)S(1)}, f32[192]{0:T(256)S(1)}, f32[192,4096]{1,0:T(8,128)}, f32[192,4096]{1,0:T(8,128)}) fusion(bf16[192,8192]{1,0:T(8,128)(2,1)} %bitcast.148, f32[192,4096]{1,0:T(8,128)} %fusion.4, f32[192]{0:T(256)S(1)} %multiply_divide_fusion, bf16[192,4096]{1,0:T(8,128)(2,1)S(1)} %copy-done.7, bf16[8192,4096]{1,0:T(8,128)(2,1)} %param.5), kind=kOutput, calls=%fused_computation.16 | convolution fusion | flops 6448742400 | bytes 47712512 | tf_op jit(solution)/shard_map/dot_general | solution.py:62
  364.1 39.2 %psum.15 = f32[192]{0:T(256)S(1)} all-reduce(f32[192]{0:T(256)S(1)} %add.236), channel_id=1, replica_groups=mesh['row'=4,'col'=8] {'row','col'}, use_global_device_ids=true, to_apply=%region_7.8 | all-reduce | flops 192 | bytes 1536 | tf_op jit(solution)/shard_map/psum | solution.py:75
  403.3 1.6 fusion.15
  405.0 1.5 fusion.16
  406.5 2.3 collective-permute-start.14
  408.9 6.6 %fusion.9 = f32[8192,128]{1,0:T(8,128)} fusion(f32[8192,128]{1,0:T(8,128)} %fusion.12, f32[192]{0:T(256)S(1)} %psum.15, bf16[8192,4096]{1,0:T(8,128)(2,1)} %param.5, bf16[192,4096]{1,0:T(8,128)(2,1)S(1)} %copy-done.7, bf16[1,192,8192]{2,1,0:T(8,128)(2,1)S(1)} %copy-done.5), kind=kOutput, calls=%fused_computation.10 | convolution fusion | flops 411566080 | bytes 13681664 | tf_op jit(solution)/shard_map/dot_general | solution.py:96
  415.6 11.8 %collective-permute-done.14 = f16[4,24,4096]{2,1,0:T(8,128)(2,1)S(1)} collective-permute-done((f16[4,24,4096]{2,1,0:T(8,128)(2,1)S(1)}, f16[4,24,4096]{2,1,0:T(8,128)(2,1)S(1)}, u32[]{:S(2)}, u32[]{:S(2)}) %collective-permute-start.14) | collective-permute-done | bytes 786464 | tf_op jit(solution)/shard_map/ppermute | solution.py:18
  427.7 0.7 collective-permute-start.15
  428.3 3.2 collective-permute-start.17
  431.6 10.9 %collective-permute-done.10 = f16[4,24,4096]{2,1,0:T(8,128)(2,1)S(1)} collective-permute-done((f16[4,24,4096]{2,1,0:T(8,128)(2,1)S(1)}, f16[4,24,4096]{2,1,0:T(8,128)(2,1)S(1)}, u32[]{:S(2)}, u32[]{:S(2)}) %collective-permute-start.10) | collective-permute-done | bytes 786464 | tf_op jit(solution)/shard_map/ppermute | solution.py:18
  442.9 0.6 collective-permute-start.11
  443.5 3.3 collective-permute-start.13
  446.9 5.7 %collective-permute-done.11 = f16[24,4096]{1,0:T(8,128)(2,1)S(1)} collective-permute-done((f16[24,4096]{1,0:T(8,128)(2,1)S(1)}, f16[24,4096]{1,0:T(8,128)(2,1)S(1)}, u32[]{:S(2)}, u32[]{:S(2)}) %collective-permute-start.11) | collective-permute-done | bytes 196640 | tf_op jit(solution)/shard_map/ppermute | solution.py:25
  452.6 0.9 collective-permute-done.13
  453.5 8.0 %collective-permute-done.12 = f16[24,4096]{1,0:T(8,128)(2,1)S(1)} collective-permute-done((f16[24,4096]{1,0:T(8,128)(2,1)S(1)}, f16[24,4096]{1,0:T(8,128)(2,1)S(1)}, u32[]{:S(2)}, u32[]{:S(2)}) %collective-permute-start.12) | collective-permute-done | bytes 196640 | tf_op jit(solution)/shard_map/ppermute | solution.py:25
  461.7 1.3 pad_maximum_fusion
  (60 shorter events, 2.8 us)
Async XLA Ops:
  7.2 1.2 copy-start
  7.2 25.9 %all-gather.7.cloned.1.call-start = ((), (), s32[]{:S(2)}) async-start(), calls=%async_computation | async-start | bytes 1966080 | tf_op jit(solution)/shard_map/all_gather | solution.py:54
  10.6 85.7 %all-gather.11.cloned.1.call-start = ((), (), s32[]{:S(2)}) async-start(), calls=%async_computation.2 | async-start | bytes 3538944 | tf_op jit(solution)/shard_map/all_gather | solution.py:41
  12.7 268.8 %all-gather.9.cloned.1.call-start = ((), (), s32[]{:S(2)}) async-start(), calls=%async_computation.1 | async-start | bytes 1966080 | tf_op jit(solution)/shard_map/all_gather | solution.py:54
  33.1 63.2 %copy-start.6 = (bf16[192,4096]{1,0:T(8,128)(2,1)S(1)}, bf16[192,4096]{1,0:T(8,128)(2,1)}, u32[]{:S(2)}) copy-start(bf16[192,4096]{1,0:T(8,128)(2,1)} %all-gather.7.cloned.1.call-done) | copy-start | bytes 4718596
  118.8 69.1 %collective-permute-start.4 = (f16[4,24,4096]{2,1,0:T(8,128)(2,1)}, f16[4,24,4096]{2,1,0:T(8,128)(2,1)S(1)}, u32[]{:S(2)}, u32[]{:S(2)}) collective-permute-start(f16[4,24,4096]{2,1,0:T(8,128)(2,1)} %fusion.14), channel_id=1, source_target_pairs={{0,1},{1,0},{2,3},{3,2},{4,5},{5,4},{6,7},{7,6},{8,9},{9,8},{10,11... | collective-permute-start | bytes 2359304 | tf_op jit(solution)/shard_map/ppermute | solution.py:18
  120.9 72.9 %collective-permute-start = (f16[4,24,4096]{2,1,0:T(8,128)(2,1)S(1)}, f16[4,24,4096]{2,1,0:T(8,128)(2,1)S(1)}, u32[]{:S(2)}, u32[]{:S(2)}) collective-permute-start(f16[4,24,4096]{2,1,0:T(8,128)(2,1)S(1)} %fusion.13), channel_id=1, source_target_pairs={{0,1},{1,0},{2,3},{3,2},{4,5},{5,4},{6,7},{7,6},{8,9},{9,8},{10,11... | collective-permute-start | bytes 2359304 | tf_op jit(solution)/shard_map/ppermute | solution.py:18
  187.9 5.9 %copy-start.2 = (f32[192,4096]{1,0:T(8,128)S(1)}, f32[192,4096]{1,0:T(8,128)}, u32[]{:S(2)}) copy-start(f32[192,4096]{1,0:T(8,128)} %get-tuple-element.18) | copy-start | bytes 9437188
  189.9 9.7 %collective-permute-start.5 = (f16[24,4096]{1,0:T(8,128)(2,1)S(1)}, f16[24,4096]{1,0:T(8,128)(2,1)S(1)}, u32[]{:S(2)}, u32[]{:S(2)}) collective-permute-start(f16[24,4096]{1,0:T(8,128)(2,1)S(1)} %get-tuple-element.37), channel_id=1, source_target_pairs={{0,2},{1,3},{2,4},{3,5},{4,6},{5,7},{6,0},{7,1},{8,10},{9,11},{10,... | collective-permute-start | bytes 589832 | tf_op jit(solution)/shard_map/ppermute | solution.py:25
  190.8 15.3 %collective-permute-start.7 = (f16[24,4096]{1,0:T(8,128)(2,1)S(1)}, f16[24,4096]{1,0:T(8,128)(2,1)S(1)}, u32[]{:S(2)}, u32[]{:S(2)}) collective-permute-start(f16[24,4096]{1,0:T(8,128)(2,1)S(1)} %get-tuple-element.38), channel_id=1, source_target_pairs={{0,6},{1,7},{2,0},{3,1},{4,2},{5,3},{6,4},{7,5},{8,14},{9,15},{10,... | collective-permute-start | bytes 589832 | tf_op jit(solution)/shard_map/ppermute | solution.py:25
  193.8 25.0 %collective-permute-start.6 = (f16[24,4096]{1,0:T(8,128)(2,1)S(1)}, f16[24,4096]{1,0:T(8,128)(2,1)S(1)}, u32[]{:S(2)}, u32[]{:S(2)}) collective-permute-start(f16[24,4096]{1,0:T(8,128)(2,1)S(1)} %get-tuple-element.39), channel_id=1, source_target_pairs={{0,4},{1,5},{2,6},{3,7},{4,0},{5,1},{6,2},{7,3},{8,12},{9,13},{10,... | collective-permute-start | bytes 589832 | tf_op jit(solution)/shard_map/ppermute | solution.py:25
  194.2 24.7 %collective-permute-start.1 = (f16[24,4096]{1,0:T(8,128)(2,1)S(1)}, f16[24,4096]{1,0:T(8,128)(2,1)S(1)}, u32[]{:S(2)}, u32[]{:S(2)}) collective-permute-start(f16[24,4096]{1,0:T(8,128)(2,1)S(1)} %get-tuple-element.34), channel_id=1, source_target_pairs={{0,2},{1,3},{2,4},{3,5},{4,6},{5,7},{6,0},{7,1},{8,10},{9,11},{10,... | collective-permute-start | bytes 589832 | tf_op jit(solution)/shard_map/ppermute | solution.py:25
  194.8 24.1 %collective-permute-start.3 = (f16[24,4096]{1,0:T(8,128)(2,1)S(1)}, f16[24,4096]{1,0:T(8,128)(2,1)S(1)}, u32[]{:S(2)}, u32[]{:S(2)}) collective-permute-start(f16[24,4096]{1,0:T(8,128)(2,1)S(1)} %get-tuple-element.35), channel_id=1, source_target_pairs={{0,6},{1,7},{2,0},{3,1},{4,2},{5,3},{6,4},{7,5},{8,14},{9,15},{10,... | collective-permute-start | bytes 589832 | tf_op jit(solution)/shard_map/ppermute | solution.py:25
  199.6 26.4 %collective-permute-start.2 = (f16[24,4096]{1,0:T(8,128)(2,1)S(1)}, f16[24,4096]{1,0:T(8,128)(2,1)S(1)}, u32[]{:S(2)}, u32[]{:S(2)}) collective-permute-start(f16[24,4096]{1,0:T(8,128)(2,1)S(1)} %get-tuple-element.36), channel_id=1, source_target_pairs={{0,4},{1,5},{2,6},{3,7},{4,0},{5,1},{6,2},{7,3},{8,12},{9,13},{10,... | collective-permute-start | bytes 589832 | tf_op jit(solution)/shard_map/ppermute | solution.py:25
  226.2 15.6 %collective-permute-start.9 = (f32[24,4096]{1,0:T(8,128)S(1)}, f32[24,4096]{1,0:T(8,128)S(1)}, u32[]{:S(2)}, u32[]{:S(2)}) collective-permute-start(f32[24,4096]{1,0:T(8,128)S(1)} %get-tuple-element.32), channel_id=1, source_target_pairs={{0,1},{1,0},{2,9},{3,8},{4,17},{5,16},{6,25},{7,24},{8,3},{9,2},{1... | collective-permute-start | bytes 1179656 | tf_op jit(solution)/shard_map/ppermute | solution.py:90
  227.7 14.2 %collective-permute-start.8 = (f32[24,4096]{1,0:T(8,128)S(1)}, f32[24,4096]{1,0:T(8,128)S(1)}, u32[]{:S(2)}, u32[]{:S(2)}) collective-permute-start(f32[24,4096]{1,0:T(8,128)S(1)} %get-tuple-element.33), channel_id=1, source_target_pairs={{0,0},{1,1},{2,8},{3,9},{4,16},{5,17},{6,24},{7,25},{8,2},{9,3},{1... | collective-permute-start | bytes 1179656 | tf_op jit(solution)/shard_map/ppermute | solution.py:90
  243.1 100.8 %all-gather.13.cloned.1.call-start = ((), (), s32[]{:S(2)}) async-start(), calls=%async_computation.3 | async-start | bytes 3538944 | tf_op jit(solution)/shard_map/all_gather | solution.py:59
  281.4 62.5 %copy-start.7 = (bf16[192,4096]{1,0:T(8,128)(2,1)S(1)}, bf16[192,4096]{1,0:T(8,128)(2,1)}, u32[]{:S(2)}) copy-start(bf16[192,4096]{1,0:T(8,128)(2,1)} %all-gather.9.cloned.1.call-done) | copy-start | bytes 4718596
  403.3 5.7 %copy-start.5 = (bf16[1,192,8192]{2,1,0:T(8,128)(2,1)S(1)}, bf16[1,192,8192]{2,1,0:T(8,128)(2,1)}, u32[]{:S(2)}) copy-start(bf16[1,192,8192]{2,1,0:T(8,128)(2,1)} %all-gather.13.cloned.1.call-done) | copy-start | bytes 9437188
  406.5 20.8 %copy-start.4 = (f32[192,4096]{1,0:T(8,128)S(1)}, f32[192,4096]{1,0:T(8,128)}, u32[]{:S(2)}) copy-start(f32[192,4096]{1,0:T(8,128)} %get-tuple-element.17) | copy-start | bytes 9437188
  406.5 20.8 %collective-permute-start.14 = (f16[4,24,4096]{2,1,0:T(8,128)(2,1)S(1)}, f16[4,24,4096]{2,1,0:T(8,128)(2,1)S(1)}, u32[]{:S(2)}, u32[]{:S(2)}) collective-permute-start(f16[4,24,4096]{2,1,0:T(8,128)(2,1)S(1)} %fusion.16), channel_id=1, source_target_pairs={{0,1},{1,0},{2,3},{3,2},{4,5},{5,4},{6,7},{7,6},{8,9},{9,8},{10,11... | collective-permute-start | bytes 2359304 | tf_op jit(solution)/shard_map/ppermute | solution.py:18
  408.9 33.6 %collective-permute-start.10 = (f16[4,24,4096]{2,1,0:T(8,128)(2,1)S(1)}, f16[4,24,4096]{2,1,0:T(8,128)(2,1)S(1)}, u32[]{:S(2)}, u32[]{:S(2)}) collective-permute-start(f16[4,24,4096]{2,1,0:T(8,128)(2,1)S(1)} %fusion.15), channel_id=1, source_target_pairs={{0,1},{1,0},{2,3},{3,2},{4,5},{5,4},{6,7},{7,6},{8,9},{9,8},{10,11... | collective-permute-start | bytes 2359304 | tf_op jit(solution)/shard_map/ppermute | solution.py:18
  415.6 26.9 %copy-start.3 = (f32[192,4096]{1,0:T(8,128)S(1)}, f32[192,4096]{1,0:T(8,128)}, u32[]{:S(2)}) copy-start(f32[192,4096]{1,0:T(8,128)} %get-tuple-element.16) | copy-start | bytes 9437188
  427.7 19.1 %collective-permute-start.15 = (f16[24,4096]{1,0:T(8,128)(2,1)S(1)}, f16[24,4096]{1,0:T(8,128)(2,1)S(1)}, u32[]{:S(2)}, u32[]{:S(2)}) collective-permute-start(f16[24,4096]{1,0:T(8,128)(2,1)S(1)} %get-tuple-element.29), channel_id=1, source_target_pairs={{0,2},{1,3},{2,4},{3,5},{4,6},{5,7},{6,0},{7,1},{8,10},{9,11},{10,... | collective-permute-start | bytes 589832 | tf_op jit(solution)/shard_map/ppermute | solution.py:25
  428.3 18.4 %collective-permute-start.17 = (f16[24,4096]{1,0:T(8,128)(2,1)S(1)}, f16[24,4096]{1,0:T(8,128)(2,1)S(1)}, u32[]{:S(2)}, u32[]{:S(2)}) collective-permute-start(f16[24,4096]{1,0:T(8,128)(2,1)S(1)} %get-tuple-element.30), channel_id=1, source_target_pairs={{0,6},{1,7},{2,0},{3,1},{4,2},{5,3},{6,4},{7,5},{8,14},{9,15},{10,... | collective-permute-start | bytes 589832 | tf_op jit(solution)/shard_map/ppermute | solution.py:25
  431.6 15.2 %collective-permute-start.16 = (f16[24,4096]{1,0:T(8,128)(2,1)S(1)}, f16[24,4096]{1,0:T(8,128)(2,1)S(1)}, u32[]{:S(2)}, u32[]{:S(2)}) collective-permute-start(f16[24,4096]{1,0:T(8,128)(2,1)S(1)} %get-tuple-element.31), channel_id=1, source_target_pairs={{0,4},{1,5},{2,6},{3,7},{4,0},{5,1},{6,2},{7,3},{8,12},{9,13},{10,... | collective-permute-start | bytes 589832 | tf_op jit(solution)/shard_map/ppermute | solution.py:25
  442.9 9.7 %collective-permute-start.11 = (f16[24,4096]{1,0:T(8,128)(2,1)S(1)}, f16[24,4096]{1,0:T(8,128)(2,1)S(1)}, u32[]{:S(2)}, u32[]{:S(2)}) collective-permute-start(f16[24,4096]{1,0:T(8,128)(2,1)S(1)} %get-tuple-element.26), channel_id=1, source_target_pairs={{0,2},{1,3},{2,4},{3,5},{4,6},{5,7},{6,0},{7,1},{8,10},{9,11},{10,... | collective-permute-start | bytes 589832 | tf_op jit(solution)/shard_map/ppermute | solution.py:25
  443.5 10.0 %collective-permute-start.13 = (f16[24,4096]{1,0:T(8,128)(2,1)S(1)}, f16[24,4096]{1,0:T(8,128)(2,1)S(1)}, u32[]{:S(2)}, u32[]{:S(2)}) collective-permute-start(f16[24,4096]{1,0:T(8,128)(2,1)S(1)} %get-tuple-element.27), channel_id=1, source_target_pairs={{0,6},{1,7},{2,0},{3,1},{4,2},{5,3},{6,4},{7,5},{8,14},{9,15},{10,... | collective-permute-start | bytes 589832 | tf_op jit(solution)/shard_map/ppermute | solution.py:25
  446.8 14.7 %collective-permute-start.12 = (f16[24,4096]{1,0:T(8,128)(2,1)S(1)}, f16[24,4096]{1,0:T(8,128)(2,1)S(1)}, u32[]{:S(2)}, u32[]{:S(2)}) collective-permute-start(f16[24,4096]{1,0:T(8,128)(2,1)S(1)} %get-tuple-element.28), channel_id=1, source_target_pairs={{0,4},{1,5},{2,6},{3,7},{4,0},{5,1},{6,2},{7,3},{8,12},{9,13},{10,... | collective-permute-start | bytes 589832 | tf_op jit(solution)/shard_map/ppermute | solution.py:25
  446.8 16.2 %copy-start.1 = (bf16[96,4096]{1,0:T(8,128)(2,1)S(1)}, bf16[96,4096]{1,0:T(8,128)(2,1)}, u32[]{:S(2)}) copy-start(bf16[96,4096]{1,0:T(8,128)(2,1)} %param.6) | copy-start | bytes 2359300
Sparse Core Ops, SparseCore 0:
  10.7 22.3 all-gather.6
  35.8 60.4 all-gather.10
  243.3 38.1 all-gather.8
  283.5 60.4 all-gather.12
where the time goes:
time: 470 us; the launch traced here: 469 us
  waiting for transfers between devices  208 us (44%)
  blocking collectives  105 us (22%)
  matrix products  98.1 us (21%)
  starting transfers between devices  29 us (6%)
  between operations  14.1 us (3%)
  other arithmetic  11.9 us (3%)
    dot_general x4, matrix products, on_device(): lax.dot_general(weighted_back, transition[rows], (((1,), (1,)), ((), ()))...  82.8 us
    psum x1, blocking collectives, on_device(): both = lax.psum(jnp.stack([norm, mass]), ('row', 'col'))  65.4 us
    all_gather x2, waiting for transfers between devices, on_device(): weighted_back = lax.all_gather(local_back, 'row', axis=0, tiled=True)  52.4 us
    all_gather x1, waiting for transfers between devices, on_device(): forward_all = [None, lax.all_gather(forward[1], 'col', axis=0, tiled=True)]  42 us
    all_gather x1, waiting for transfers between devices, on_device(): forward_all[0] = lax.all_gather(forward[0], 'col', axis=0, tiled=True)  41.2 us
    psum x1, blocking collectives, on_device(): normal_all = lax.psum(norm, ('row', 'col'))  39.2 us
    ppermute x12, waiting for transfers between devices, reduce_scatter(): lax.ppermute(piece, 'col', [(c, (c + 2 * k) % col_count) for c in range(c...  35.8 us
    ppermute x4, waiting for transfers between devices, reduce_scatter(): got = lax.ppermute(away, 'col', [(c, c ^ 1) for c in range(col_count)])  22.7 us
  transfers between devices with their start and end apart: 22, of which 13 were waited for; matrix products, arithmetic and copies ran while one was open for 13% of the time, Pallas kernels for 0%

commit v1 on v0

--- a/solution.py
+++ b/solution.py
@@ -7,6 +7,41 @@
 N = 192
 DW = 128
 CHUNKS = 2
+
+
+def heaps_obtain(inner_x, axis_key):
+    built = lax.axis_size(axis_key)
+    arr_out, front, even = (built, lax.axis_index(axis_key), inner_x.shape[0])
+    pile = []
+    for dd, j in enumerate(inner_x.shape):
+        pile.append(j * arr_out if dd == 0 else j)
+    local_now = lax.dynamic_update_slice_in_dim(
+        jnp.zeros(pile, inner_x.dtype), inner_x, front * even, axis=0
+    )
+    new = parts_out = inner_x
+    no = 1
+    while no < arr_out // 2 + 1:
+        views = []
+        dd = 0
+        while dd < arr_out:
+            views.append((dd, (dd + 1) % arr_out))
+            dd += 1
+        new = lax.ppermute(new, axis_name=axis_key, perm=views)
+        local_now = lax.dynamic_update_slice_in_dim(
+            local_now, new, (front - no) % arr_out * even, axis=0
+        )
+        if 2 * no < arr_out:
+            cards = []
+            dd = 0
+            while dd < arr_out:
+                cards.append((dd, (dd - 1) % arr_out))
+                dd = dd + 1
+            parts_out = lax.ppermute(parts_out, axis_key, cards)
+            local_now = lax.dynamic_update_slice_in_dim(
+                local_now, parts_out, (front + no) % arr_out * even, axis=0
+            )
+        no = no + 1
+    return local_now
 
 
 def reduce_scatter(partial, scale, col_count, col_index, local_seqs):
@@ -38,7 +73,7 @@
     block_src = transition.shape[0]
     block_dst = transition.shape[1]
     seq_total = local_seqs * col_count
-    forward_all = [None, lax.all_gather(forward[1], "col", axis=0, tiled=True)]
+    forward_all = [None, heaps_obtain(forward[1], "col")]
     columns = lax.broadcasted_iota(jnp.int32, (row_seqs, emission.shape[0]), 1)
     window = transition[:, :DW]
     totals = jnp.zeros((block_src, DW), jnp.float32)

time: 470 us -> 491 us (1.045)
  waiting for transfers between devices: 208 us -> 173 us
  starting transfers between devices: 29 us -> 57.7 us
  blocking collectives: 105 us -> 129 us
  matrix products: 98.1 us -> 89.2 us
  local copies, waits for them, and re-layouts: 3.78 us -> 11.9 us
    all_gather x1 -> x0, waiting for transfers between devices: 42 us -> none  [on_device(): forward_all = [None, lax.all_gather(forward[1], 'col', axis=0, tiled=True)]]
    ppermute x0 -> x7, waiting for transfers between devices: none -> 37.9 us  [the longest x4 37.9 us: heaps_obtain(): new = lax.ppermute(new, axis_name=axis_key, perm=views)]
    psum x1, blocking collectives: 39.2 us -> 66.1 us  [on_device(): normal_all = lax.psum(norm, ('row', 'col'))]
    ppermute x4, waiting for transfers between devices: 22.7 us -> 0.01 us  [reduce_scatter(): got = lax.ppermute(away, 'col', [(c, c ^ 1) for c in range(col_count)])]
    ppermute x0 -> x7, starting transfers between devices: none -> 19.5 us  [the longest x4 10.4 us: heaps_obtain(): new = lax.ppermute(new, axis_name=axis_key, perm=views)]
    ppermute x12, starting transfers between devices: 22.1 us -> 31.7 us  [reduce_scatter(): lax.ppermute(piece, 'col', [(c, (c + 2 * k) % col_count) for c in range(c...]
    ppermute x2, waiting for transfers between devices: 13.4 us -> 6.39 us  [on_device(): arrived.append(lax.ppermute(part, ('row', 'col'), moves))]
    dot_general x4, matrix products: 82.8 us -> 76.3 us  [on_device(): lax.dot_general(weighted_back, transition[rows], (((1,), (1,)), ((), ()))...]
  transfers between devices with their start and end apart: 22 -> 28, of which waited for: 13 -> 12; matrix products, arithmetic and copies ran while one was open for 13% -> 10% of each run, Pallas kernels for 0% -> 0%
where the time goes in v1:
time: 491 us; the launch traced here: 490 us
  waiting for transfers between devices  173 us (35%)
  blocking collectives  129 us (26%)
  matrix products  89.2 us (18%)
  starting transfers between devices  57.7 us (12%)
  other arithmetic  15.2 us (3%)
  between operations  14 us (3%)
  local copies, waits for them, and re-layouts  11.9 us (2%)
    dot_general x4, matrix products, on_device(): lax.dot_general(weighted_back, transition[rows], (((1,), (1,)), ((), ()))...  76.3 us
    psum x1, blocking collectives, on_device(): normal_all = lax.psum(norm, ('row', 'col'))  66.1 us
    psum x1, blocking collectives, on_device(): both = lax.psum(jnp.stack([norm, mass]), ('row', 'col'))  62.6 us
    all_gather x2, waiting for transfers between devices, on_device(): weighted_back = lax.all_gather(local_back, 'row', axis=0, tiled=True)  46.5 us
    all_gather x1, waiting for transfers between devices, on_device(): forward_all[0] = lax.all_gather(forward[0], 'col', axis=0, tiled=True)  44.2 us
    ppermute x4, waiting for transfers between devices, heaps_obtain(): new = lax.ppermute(new, axis_name=axis_key, perm=views)  37.9 us
    ppermute x12, waiting for transfers between devices, reduce_scatter(): lax.ppermute(piece, 'col', [(c, (c + 2 * k) % col_count) for c in range(c...  37.7 us
    ppermute x12, starting transfers between devices, reduce_scatter(): lax.ppermute(piece, 'col', [(c, (c + 2 * k) % col_count) for c in range(c...  31.7 us
  transfers between devices with their start and end apart: 28, of which 12 were waited for; matrix products, arithmetic and copies ran while one was open for 10% of the time, Pallas kernels for 0%

profile of v1, /device:TPU:0, one launch (start us, length us, event | category | flops | bytes accessed | tf_op | source)
XLA Modules:
  0.0 490.0 jit_solution(12077105299841465130)
XLA Ops:
  7.2 2.0 fusion.49
  9.3 2.9 collective-permute-start.8
  12.2 3.0 collective-permute-start.9
  16.1 2.2 fusion.10
  18.3 2.1 broadcast_in_dim.2
  21.2 7.8 %collective-permute-done.8 = bf16[24,8192]{1,0:T(8,128)(2,1)S(1)} collective-permute-done((bf16[24,8192]{1,0:T(8,128)(2,1)S(1)}, bf16[24,8192]{1,0:T(8,128)(2,1)S(1)}, u32[]{:S(2)}, u32[]{:S(2)}) %collective-permute-start.8) | collective-permute-done | bytes 393248 | tf_op jit(solution)/shard_map/ppermute | solution.py:29
  29.0 2.5 collective-permute-start.10
  31.5 3.0 collective-permute-start.11
  36.1 11.4 %collective-permute-done.10 = bf16[24,8192]{1,0:T(8,128)(2,1)S(1)} collective-permute-done((bf16[24,8192]{1,0:T(8,128)(2,1)S(1)}, bf16[24,8192]{1,0:T(8,128)(2,1)S(1)}, u32[]{:S(2)}, u32[]{:S(2)}) %collective-permute-start.10) | collective-permute-done | bytes 393248 | tf_op jit(solution)/shard_map/ppermute | solution.py:29
  47.5 2.5 collective-permute-start.12
  50.0 3.0 collective-permute-start.13
  54.6 10.5 %collective-permute-done.12 = bf16[24,8192]{1,0:T(8,128)(2,1)S(1)} collective-permute-done((bf16[24,8192]{1,0:T(8,128)(2,1)S(1)}, bf16[24,8192]{1,0:T(8,128)(2,1)S(1)}, u32[]{:S(2)}, u32[]{:S(2)}) %collective-permute-start.12) | collective-permute-done | bytes 393248 | tf_op jit(solution)/shard_map/ppermute | solution.py:29
  65.1 2.5 collective-permute-start.14
  69.2 8.1 %collective-permute-done.14 = bf16[24,8192]{1,0:T(8,128)(2,1)S(1)} collective-permute-done((bf16[24,8192]{1,0:T(8,128)(2,1)S(1)}, bf16[24,8192]{1,0:T(8,128)(2,1)S(1)}, u32[]{:S(2)}, u32[]{:S(2)}) %collective-permute-start.14) | collective-permute-done | bytes 393248 | tf_op jit(solution)/shard_map/ppermute | solution.py:29
  78.2 18.3 %fusion.6 = f32[192,4096]{1,0:T(8,128)} fusion(bf16[192,4096]{1,0:T(8,128)(2,1)} %all-gather.5.cloned.1.call-done, bf16[8192,4096]{1,0:T(8,128)(2,1)} %param.5), kind=kOutput, calls=%fused_computation.6 | convolution fusion | flops 6442450944 | bytes 38273024 | tf_op jit(solution)/shard_map/dot_general | solution.py:97
  96.5 20.1 %multiply_reduce_fusion.2 = (f32[192]{0:T(256)S(1)}, f32[192]{0:T(256)S(1)}, f32[192]{0:T(256)S(1)}, f32[192]{0:T(256)S(1)}, f32[192,4096]{1,0:T(8,128)}, /*index=5*/f32[192,4096]{1,0:T(8,128)}) fusion(bf16[192,8192]{1,0:T(8,128)(2,1)} %constant_dynamic-update-slice_fusion, f32[192,4096]{1,0:T(8,128)} %fusion.6, bf16[192,4096]{1,0:T(8,128)(2,1)S(1)} %copy-done.6, ...), kind=kOutput, calls=%fused_computation.18 | convolution fusion | flops 6450315264 | bytes 47713280 | tf_op jit(solution)/shard_map/dot_general | solution.py:97
  116.6 2.4 fusion.14
  119.0 1.5 fusion.13
  120.5 2.1 collective-permute-start
  122.6 62.6 %psum.14 = f32[2,192]{1,0:T(2,128)S(1)} all-reduce(f32[2,192]{1,0:T(2,128)S(1)} %pad_maximum_fusion.1), channel_id=1, replica_groups=mesh['row'=4,'col'=8] {'row','col'}, use_global_device_ids=true, to_apply=%region_4.5 | all-reduce | flops 384 | bytes 3072 | tf_op jit(solution)/shard_map/psum | solution.py:107
  185.2 1.8 fusion.48
  187.2 1.9 collective-permute-start.7
  190.8 3.2 collective-permute-start.3
  195.1 9.3 %collective-permute-start.1 = (f16[24,4096]{1,0:T(8,128)(2,1)S(1)}, f16[24,4096]{1,0:T(8,128)(2,1)S(1)}, u32[]{:S(2)}, u32[]{:S(2)}) collective-permute-start(f16[24,4096]{1,0:T(8,128)(2,1)S(1)} %get-tuple-element.34), channel_id=1, source_target_pairs={{0,2},{1,3},{2,4},{3,5},{4,6},{5,7},{6,0},{7,1},{8,10},{9,11},{10,... | collective-permute-start | bytes 589832 | tf_op jit(solution)/shard_map/ppermute | solution.py:60
  204.4 12.2 %collective-permute-done.6 = f16[24,4096]{1,0:T(8,128)(2,1)S(1)} collective-permute-done((f16[24,4096]{1,0:T(8,128)(2,1)S(1)}, f16[24,4096]{1,0:T(8,128)(2,1)S(1)}, u32[]{:S(2)}, u32[]{:S(2)}) %collective-permute-start.6) | collective-permute-done | bytes 196640 | tf_op jit(solution)/shard_map/ppermute | solution.py:60
  216.7 6.3 %collective-permute-done.2 = f16[24,4096]{1,0:T(8,128)(2,1)S(1)} collective-permute-done((f16[24,4096]{1,0:T(8,128)(2,1)S(1)}, f16[24,4096]{1,0:T(8,128)(2,1)S(1)}, u32[]{:S(2)}, u32[]{:S(2)}) %collective-permute-start.2) | collective-permute-done | bytes 196640 | tf_op jit(solution)/shard_map/ppermute | solution.py:60
  224.0 1.4 collective-permute-start.16
  225.5 6.4 %collective-permute-done.16 = f32[24,4096]{1,0:T(8,128)S(1)} collective-permute-done((f32[24,4096]{1,0:T(8,128)S(1)}, f32[24,4096]{1,0:T(8,128)S(1)}, u32[]{:S(2)}, u32[]{:S(2)}) %collective-permute-start.16) | collective-permute-done | bytes 393248 | tf_op jit(solution)/shard_map/ppermute | solution.py:125
  232.0 1.1 fusion.20
  233.9 1.0 maximum_divide_fusion.2
  234.9 46.5 %all-gather.7.cloned.1.call-done = bf16[192,4096]{1,0:T(8,128)(2,1)} async-done(((bf16[48,4096]{1,0:T(8,128)(2,1)}), bf16[192,4096]{1,0:T(8,128)(2,1)}) %all-gather.7.cloned.1.call-update) | async-done | bytes 1572880 | tf_op jit(solution)/shard_map/all_gather | solution.py:89
  281.4 18.5 %fusion.4 = f32[192,4096]{1,0:T(8,128)} fusion(bf16[192,4096]{1,0:T(8,128)(2,1)} %all-gather.7.cloned.1.call-done, bf16[8192,4096]{1,0:T(8,128)(2,1)} %param.5), kind=kOutput, calls=%fused_computation.4 | convolution fusion | flops 6442450944 | bytes 38273024 | tf_op jit(solution)/shard_map/dot_general | solution.py:97
  299.9 44.2 %all-gather.9.cloned.1.call-done = bf16[1,192,8192]{2,1,0:T(8,128)(2,1)} async-done(((bf16[1,24,8192]{2,1,0:T(8,128)(2,1)}), bf16[1,192,8192]{2,1,0:T(8,128)(2,1)}) %all-gather.9.cloned.1.call-update) | async-done | bytes 3145744 | tf_op jit(solution)/shard_map/all_gather | solution.py:94
  344.1 19.4 %multiply_reduce_fusion = (f32[192]{0:T(256)S(1)}, f32[192]{0:T(256)S(1)}, f32[192,4096]{1,0:T(8,128)S(1)}, f32[192,4096]{1,0:T(8,128)}) fusion(bf16[192,8192]{1,0:T(8,128)(2,1)} %bitcast.146, f32[192,4096]{1,0:T(8,128)} %fusion.4, f32[192]{0:T(256)S(1)} %multiply_divide_fusion, bf16[192,4096]{1,0:T(8,128)(2,1)} %all-gather.7.cloned.1.call-done, ...), kind=kOutput, calls=%fused_computation.16 | convolution fusion | flops 6448742400 | bytes 47712512 | tf_op jit(solution)/shard_map/dot_general | solution.py:97
  363.5 2.4 fusion.16
  366.4 1.0 fusion.15
  367.4 1.5 collective-permute-start.17
  368.9 66.1 %psum.15 = f32[192]{0:T(256)S(1)} all-reduce(f32[192]{0:T(256)S(1)} %add.306), channel_id=1, replica_groups=mesh['row'=4,'col'=8] {'row','col'}, use_global_device_ids=true, to_apply=%region_7.8 | all-reduce | flops 192 | bytes 1536 | tf_op jit(solution)/shard_map/psum | solution.py:110
  435.0 3.4 fusion.12
  438.4 6.3 %fusion.9 = f32[8192,128]{1,0:T(8,128)} fusion(f32[8192,128]{1,0:T(8,128)S(1)} %fusion.12, bf16[192,8192]{1,0:T(8,128)(2,1)} %constant_dynamic-update-slice_fusion, f32[192]{0:T(256)S(1)} %bitcast.142, bf16[8192,4096]{1,0:T(8,128)(2,1)} %param.5, bf16[192,4096]{1,0:T(8,128)(2,1)} %all-gather.5.cloned.1.call-done), kind=kOutput, calls=%fused_computation.10 | convolution fusion | flops 411566080 | bytes 13681408 | tf_op jit(solution)/shard_map/dot_general | solution.py:131
  444.8 1.4 fusion.46
  446.3 1.6 collective-permute-start.24
  449.3 1.4 fusion.45
  450.8 3.2 collective-permute-start.20
  454.4 8.9 %collective-permute-start.18 = (f16[24,4096]{1,0:T(8,128)(2,1)S(1)}, f16[24,4096]{1,0:T(8,128)(2,1)S(1)}, u32[]{:S(2)}, u32[]{:S(2)}) collective-permute-start(f16[24,4096]{1,0:T(8,128)(2,1)S(1)} %get-tuple-element.26), channel_id=1, source_target_pairs={{0,2},{1,3},{2,4},{3,5},{4,6},{5,7},{6,0},{7,1},{8,10},{9,11},{10,... | collective-permute-start | bytes 589832 | tf_op jit(solution)/shard_map/ppermute | solution.py:60
  463.3 12.2 %collective-permute-done.23 = f16[24,4096]{1,0:T(8,128)(2,1)S(1)} collective-permute-done((f16[24,4096]{1,0:T(8,128)(2,1)S(1)}, f16[24,4096]{1,0:T(8,128)(2,1)S(1)}, u32[]{:S(2)}, u32[]{:S(2)}) %collective-permute-start.23) | collective-permute-done | bytes 196640 | tf_op jit(solution)/shard_map/ppermute | solution.py:60
  475.6 6.3 %collective-permute-done.19 = f16[24,4096]{1,0:T(8,128)(2,1)S(1)} collective-permute-done((f16[24,4096]{1,0:T(8,128)(2,1)S(1)}, f16[24,4096]{1,0:T(8,128)(2,1)S(1)}, u32[]{:S(2)}, u32[]{:S(2)}) %collective-permute-start.19) | collective-permute-done | bytes 196640 | tf_op jit(solution)/shard_map/ppermute | solution.py:60
  482.2 1.3 pad_maximum_fusion
  (78 shorter events, 15.3 us)
Async XLA Ops:
  7.2 8.9 %copy-start = (bf16[96,4096]{1,0:T(8,128)(2,1)S(1)}, bf16[96,4096]{1,0:T(8,128)(2,1)}, u32[]{:S(2)}) copy-start(bf16[96,4096]{1,0:T(8,128)(2,1)} %param.6) | copy-start | bytes 2359300
  7.2 71.0 %all-gather.5.cloned.1.call-start = ((), (), s32[]{:S(2)}) async-start(), calls=%async_computation | async-start | bytes 1966080 | tf_op jit(solution)/shard_map/all_gather | solution.py:89
  9.2 11.2 %copy-start.5 = (bf16[2,24,8192]{2,1,0:T(8,128)(2,1)S(1)}, bf16[2,24,8192]{2,1,0:T(8,128)(2,1)}, u32[]{:S(2)}) copy-start(bf16[2,24,8192]{2,1,0:T(8,128)(2,1)} %param.8) | copy-start | bytes 2359300
  9.3 19.7 %collective-permute-start.8 = (bf16[24,8192]{1,0:T(8,128)(2,1)S(1)}, bf16[24,8192]{1,0:T(8,128)(2,1)S(1)}, u32[]{:S(2)}, u32[]{:S(2)}) collective-permute-start(bf16[24,8192]{1,0:T(8,128)(2,1)S(1)} %get-tuple-element.25), channel_id=1, source_target_pairs={{0,1},{1,2},{2,3},{3,4},{4,5},{5,6},{6,7},{7,0},{8,9},{9,10},{10,1... | collective-permute-start | bytes 1179656 | tf_op jit(solution)/shard_map/ppermute | solution.py:29
  12.2 19.3 %collective-permute-start.9 = (bf16[24,8192]{1,0:T(8,128)(2,1)S(1)}, bf16[24,8192]{1,0:T(8,128)(2,1)S(1)}, u32[]{:S(2)}, u32[]{:S(2)}) collective-permute-start(bf16[24,8192]{1,0:T(8,128)(2,1)S(1)} %get-tuple-element.25), channel_id=1, source_target_pairs={{0,7},{1,0},{2,1},{3,2},{4,3},{5,4},{6,5},{7,6},{8,15},{9,8},{10,9... | collective-permute-start | bytes 1179656 | tf_op jit(solution)/shard_map/ppermute | solution.py:39
  18.3 263.1 %all-gather.7.cloned.1.call-start = ((), (), s32[]{:S(2)}) async-start(), calls=%async_computation.1 | async-start | bytes 1966080 | tf_op jit(solution)/shard_map/all_gather | solution.py:89
  29.0 18.5 %collective-permute-start.10 = (bf16[24,8192]{1,0:T(8,128)(2,1)S(1)}, bf16[24,8192]{1,0:T(8,128)(2,1)S(1)}, u32[]{:S(2)}, u32[]{:S(2)}) collective-permute-start(bf16[24,8192]{1,0:T(8,128)(2,1)S(1)} %collective-permute-done.8), channel_id=1, source_target_pairs={{0,1},{1,2},{2,3},{3,4},{4,5},{5,6},{6,7},{7,0},{8,9},{9,10},{10,1... | collective-permute-start | bytes 1179656 | tf_op jit(solution)/shard_map/ppermute | solution.py:29
  31.5 18.5 %collective-permute-start.11 = (bf16[24,8192]{1,0:T(8,128)(2,1)S(1)}, bf16[24,8192]{1,0:T(8,128)(2,1)S(1)}, u32[]{:S(2)}, u32[]{:S(2)}) collective-permute-start(bf16[24,8192]{1,0:T(8,128)(2,1)S(1)} %collective-permute-done.9), channel_id=1, source_target_pairs={{0,7},{1,0},{2,1},{3,2},{4,3},{5,4},{6,5},{7,6},{8,15},{9,8},{10,9... | collective-permute-start | bytes 1179656 | tf_op jit(solution)/shard_map/ppermute | solution.py:39
  47.5 17.6 %collective-permute-start.12 = (bf16[24,8192]{1,0:T(8,128)(2,1)S(1)}, bf16[24,8192]{1,0:T(8,128)(2,1)S(1)}, u32[]{:S(2)}, u32[]{:S(2)}) collective-permute-start(bf16[24,8192]{1,0:T(8,128)(2,1)S(1)} %collective-permute-done.10), channel_id=1, source_target_pairs={{0,1},{1,2},{2,3},{3,4},{4,5},{5,6},{6,7},{7,0},{8,9},{9,10},{10,1... | collective-permute-start | bytes 1179656 | tf_op jit(solution)/shard_map/ppermute | solution.py:29
  50.0 18.4 %collective-permute-start.13 = (bf16[24,8192]{1,0:T(8,128)(2,1)S(1)}, bf16[24,8192]{1,0:T(8,128)(2,1)S(1)}, u32[]{:S(2)}, u32[]{:S(2)}) collective-permute-start(bf16[24,8192]{1,0:T(8,128)(2,1)S(1)} %collective-permute-done.11), channel_id=1, source_target_pairs={{0,7},{1,0},{2,1},{3,2},{4,3},{5,4},{6,5},{7,6},{8,15},{9,8},{10,9... | collective-permute-start | bytes 1179656 | tf_op jit(solution)/shard_map/ppermute | solution.py:39
  65.1 12.2 %collective-permute-start.14 = (bf16[24,8192]{1,0:T(8,128)(2,1)S(1)}, bf16[24,8192]{1,0:T(8,128)(2,1)S(1)}, u32[]{:S(2)}, u32[]{:S(2)}) collective-permute-start(bf16[24,8192]{1,0:T(8,128)(2,1)S(1)} %collective-permute-done.12), channel_id=1, source_target_pairs={{0,1},{1,2},{2,3},{3,4},{4,5},{5,6},{6,7},{7,0},{8,9},{9,10},{10,1... | collective-permute-start | bytes 1179656 | tf_op jit(solution)/shard_map/ppermute | solution.py:29
  78.2 18.3 %copy-start.6 = (bf16[192,4096]{1,0:T(8,128)(2,1)S(1)}, bf16[192,4096]{1,0:T(8,128)(2,1)}, u32[]{:S(2)}) copy-start(bf16[192,4096]{1,0:T(8,128)(2,1)} %all-gather.5.cloned.1.call-done) | copy-start | bytes 4718596
  119.0 66.3 %collective-permute-start.4 = (f16[4,24,4096]{2,1,0:T(8,128)(2,1)}, f16[4,24,4096]{2,1,0:T(8,128)(2,1)S(1)}, u32[]{:S(2)}, u32[]{:S(2)}) collective-permute-start(f16[4,24,4096]{2,1,0:T(8,128)(2,1)} %fusion.14), channel_id=1, source_target_pairs={{0,1},{1,0},{2,3},{3,2},{4,5},{5,4},{6,7},{7,6},{8,9},{9,8},{10,11... | collective-permute-start | bytes 2359304 | tf_op jit(solution)/shard_map/ppermute | solution.py:53
  120.5 69.9 %collective-permute-start = (f16[4,24,4096]{2,1,0:T(8,128)(2,1)S(1)}, f16[4,24,4096]{2,1,0:T(8,128)(2,1)S(1)}, u32[]{:S(2)}, u32[]{:S(2)}) collective-permute-start(f16[4,24,4096]{2,1,0:T(8,128)(2,1)S(1)} %fusion.13), channel_id=1, source_target_pairs={{0,1},{1,0},{2,3},{3,2},{4,5},{5,4},{6,7},{7,6},{8,9},{9,8},{10,11... | collective-permute-start | bytes 2359304 | tf_op jit(solution)/shard_map/ppermute | solution.py:53
  185.2 5.2 %copy-start.2 = (f32[192,4096]{1,0:T(8,128)S(1)}, f32[192,4096]{1,0:T(8,128)}, u32[]{:S(2)}) copy-start(f32[192,4096]{1,0:T(8,128)} %get-tuple-element.18) | copy-start | bytes 9437188
  187.2 7.9 %collective-permute-start.7 = (f16[24,4096]{1,0:T(8,128)(2,1)S(1)}, f16[24,4096]{1,0:T(8,128)(2,1)S(1)}, u32[]{:S(2)}, u32[]{:S(2)}) collective-permute-start(f16[24,4096]{1,0:T(8,128)(2,1)S(1)} %get-tuple-element.38), channel_id=1, source_target_pairs={{0,6},{1,7},{2,0},{3,1},{4,2},{5,3},{6,4},{7,5},{8,14},{9,15},{10,... | collective-permute-start | bytes 589832 | tf_op jit(solution)/shard_map/ppermute | solution.py:60
  189.0 27.6 %collective-permute-start.6 = (f16[24,4096]{1,0:T(8,128)(2,1)S(1)}, f16[24,4096]{1,0:T(8,128)(2,1)S(1)}, u32[]{:S(2)}, u32[]{:S(2)}) collective-permute-start(f16[24,4096]{1,0:T(8,128)(2,1)S(1)} %get-tuple-element.39), channel_id=1, source_target_pairs={{0,4},{1,5},{2,6},{3,7},{4,0},{5,1},{6,2},{7,3},{8,12},{9,13},{10,... | collective-permute-start | bytes 589832 | tf_op jit(solution)/shard_map/ppermute | solution.py:60
  189.7 26.9 %collective-permute-start.5 = (f16[24,4096]{1,0:T(8,128)(2,1)S(1)}, f16[24,4096]{1,0:T(8,128)(2,1)S(1)}, u32[]{:S(2)}, u32[]{:S(2)}) collective-permute-start(f16[24,4096]{1,0:T(8,128)(2,1)S(1)} %get-tuple-element.37), channel_id=1, source_target_pairs={{0,2},{1,3},{2,4},{3,5},{4,6},{5,7},{6,0},{7,1},{8,10},{9,11},{10,... | collective-permute-start | bytes 589832 | tf_op jit(solution)/shard_map/ppermute | solution.py:60
  190.8 25.9 %collective-permute-start.3 = (f16[24,4096]{1,0:T(8,128)(2,1)S(1)}, f16[24,4096]{1,0:T(8,128)(2,1)S(1)}, u32[]{:S(2)}, u32[]{:S(2)}) collective-permute-start(f16[24,4096]{1,0:T(8,128)(2,1)S(1)} %get-tuple-element.35), channel_id=1, source_target_pairs={{0,6},{1,7},{2,0},{3,1},{4,2},{5,3},{6,4},{7,5},{8,14},{9,15},{10,... | collective-permute-start | bytes 589832 | tf_op jit(solution)/shard_map/ppermute | solution.py:60
  194.0 29.0 %collective-permute-start.2 = (f16[24,4096]{1,0:T(8,128)(2,1)S(1)}, f16[24,4096]{1,0:T(8,128)(2,1)S(1)}, u32[]{:S(2)}, u32[]{:S(2)}) collective-permute-start(f16[24,4096]{1,0:T(8,128)(2,1)S(1)} %get-tuple-element.36), channel_id=1, source_target_pairs={{0,4},{1,5},{2,6},{3,7},{4,0},{5,1},{6,2},{7,3},{8,12},{9,13},{10,... | collective-permute-start | bytes 589832 | tf_op jit(solution)/shard_map/ppermute | solution.py:60
  195.1 27.9 %collective-permute-start.1 = (f16[24,4096]{1,0:T(8,128)(2,1)S(1)}, f16[24,4096]{1,0:T(8,128)(2,1)S(1)}, u32[]{:S(2)}, u32[]{:S(2)}) collective-permute-start(f16[24,4096]{1,0:T(8,128)(2,1)S(1)} %get-tuple-element.34), channel_id=1, source_target_pairs={{0,2},{1,3},{2,4},{3,5},{4,6},{5,7},{6,0},{7,1},{8,10},{9,11},{10,... | collective-permute-start | bytes 589832 | tf_op jit(solution)/shard_map/ppermute | solution.py:60
  223.3 2.2 collective-permute-start.15
  224.0 7.8 %collective-permute-start.16 = (f32[24,4096]{1,0:T(8,128)S(1)}, f32[24,4096]{1,0:T(8,128)S(1)}, u32[]{:S(2)}, u32[]{:S(2)}) collective-permute-start(f32[24,4096]{1,0:T(8,128)S(1)} %get-tuple-element.32), channel_id=1, source_target_pairs={{0,1},{1,0},{2,9},{3,8},{4,17},{5,16},{6,25},{7,24},{8,3},{9,2},{1... | collective-permute-start | bytes 1179656 | tf_op jit(solution)/shard_map/ppermute | solution.py:125
  233.1 110.9 %all-gather.9.cloned.1.call-start = ((), (), s32[]{:S(2)}) async-start(), calls=%async_computation.2 | async-start | bytes 3538944 | tf_op jit(solution)/shard_map/all_gather | solution.py:94
  365.8 78.9 %collective-permute-start.21 = (f16[4,24,4096]{2,1,0:T(8,128)(2,1)}, f16[4,24,4096]{2,1,0:T(8,128)(2,1)}, u32[]{:S(2)}, u32[]{:S(2)}) collective-permute-start(f16[4,24,4096]{2,1,0:T(8,128)(2,1)} %fusion.16), channel_id=1, source_target_pairs={{0,1},{1,0},{2,3},{3,2},{4,5},{5,4},{6,7},{7,6},{8,9},{9,8},{10,11... | collective-permute-start | bytes 2359304 | tf_op jit(solution)/shard_map/ppermute | solution.py:53
  367.4 81.9 %collective-permute-start.17 = (f16[4,24,4096]{2,1,0:T(8,128)(2,1)}, f16[4,24,4096]{2,1,0:T(8,128)(2,1)}, u32[]{:S(2)}, u32[]{:S(2)}) collective-permute-start(f16[4,24,4096]{2,1,0:T(8,128)(2,1)} %fusion.15), channel_id=1, source_target_pairs={{0,1},{1,0},{2,3},{3,2},{4,5},{5,4},{6,7},{7,6},{8,9},{9,8},{10,11... | collective-permute-start | bytes 2359304 | tf_op jit(solution)/shard_map/ppermute | solution.py:53
  438.4 6.3 %copy-start.3 = (f32[192,4096]{1,0:T(8,128)S(1)}, f32[192,4096]{1,0:T(8,128)}, u32[]{:S(2)}) copy-start(f32[192,4096]{1,0:T(8,128)} %get-tuple-element.17) | copy-start | bytes 9437188
  446.3 8.1 %collective-permute-start.24 = (f16[24,4096]{1,0:T(8,128)(2,1)S(1)}, f16[24,4096]{1,0:T(8,128)(2,1)S(1)}, u32[]{:S(2)}, u32[]{:S(2)}) collective-permute-start(f16[24,4096]{1,0:T(8,128)(2,1)S(1)} %get-tuple-element.30), channel_id=1, source_target_pairs={{0,6},{1,7},{2,0},{3,1},{4,2},{5,3},{6,4},{7,5},{8,14},{9,15},{10,... | collective-permute-start | bytes 589832 | tf_op jit(solution)/shard_map/ppermute | solution.py:60
  447.9 27.7 %collective-permute-start.23 = (f16[24,4096]{1,0:T(8,128)(2,1)S(1)}, f16[24,4096]{1,0:T(8,128)(2,1)S(1)}, u32[]{:S(2)}, u32[]{:S(2)}) collective-permute-start(f16[24,4096]{1,0:T(8,128)(2,1)S(1)} %get-tuple-element.31), channel_id=1, source_target_pairs={{0,4},{1,5},{2,6},{3,7},{4,0},{5,1},{6,2},{7,3},{8,12},{9,13},{10,... | collective-permute-start | bytes 589832 | tf_op jit(solution)/shard_map/ppermute | solution.py:60
  448.6 26.9 %collective-permute-start.22 = (f16[24,4096]{1,0:T(8,128)(2,1)S(1)}, f16[24,4096]{1,0:T(8,128)(2,1)S(1)}, u32[]{:S(2)}, u32[]{:S(2)}) collective-permute-start(f16[24,4096]{1,0:T(8,128)(2,1)S(1)} %get-tuple-element.29), channel_id=1, source_target_pairs={{0,2},{1,3},{2,4},{3,5},{4,6},{5,7},{6,0},{7,1},{8,10},{9,11},{10,... | collective-permute-start | bytes 589832 | tf_op jit(solution)/shard_map/ppermute | solution.py:60
  450.7 31.5 %copy-start.4 = (f32[1,24,8192]{2,1,0:T(8,128)S(1)}, f32[1,24,8192]{2,1,0:T(8,128)}, u32[]{:S(2)}) copy-start(f32[1,24,8192]{2,1,0:T(8,128)} %maximum_divide_fusion.2) | copy-start | bytes 2359300
  450.8 24.8 %collective-permute-start.20 = (f16[24,4096]{1,0:T(8,128)(2,1)S(1)}, f16[24,4096]{1,0:T(8,128)(2,1)S(1)}, u32[]{:S(2)}, u32[]{:S(2)}) collective-permute-start(f16[24,4096]{1,0:T(8,128)(2,1)S(1)} %get-tuple-element.27), channel_id=1, source_target_pairs={{0,6},{1,7},{2,0},{3,1},{4,2},{5,3},{6,4},{7,5},{8,14},{9,15},{10,... | collective-permute-start | bytes 589832 | tf_op jit(solution)/shard_map/ppermute | solution.py:60
  454.0 27.9 %collective-permute-start.19 = (f16[24,4096]{1,0:T(8,128)(2,1)S(1)}, f16[24,4096]{1,0:T(8,128)(2,1)S(1)}, u32[]{:S(2)}, u32[]{:S(2)}) collective-permute-start(f16[24,4096]{1,0:T(8,128)(2,1)S(1)} %get-tuple-element.28), channel_id=1, source_target_pairs={{0,4},{1,5},{2,6},{3,7},{4,0},{5,1},{6,2},{7,3},{8,12},{9,13},{10,... | collective-permute-start | bytes 589832 | tf_op jit(solution)/shard_map/ppermute | solution.py:60
  454.4 27.6 %collective-permute-start.18 = (f16[24,4096]{1,0:T(8,128)(2,1)S(1)}, f16[24,4096]{1,0:T(8,128)(2,1)S(1)}, u32[]{:S(2)}, u32[]{:S(2)}) collective-permute-start(f16[24,4096]{1,0:T(8,128)(2,1)S(1)} %get-tuple-element.26), channel_id=1, source_target_pairs={{0,2},{1,3},{2,4},{3,5},{4,6},{5,7},{6,0},{7,1},{8,10},{9,11},{10,... | collective-permute-start | bytes 589832 | tf_op jit(solution)/shard_map/ppermute | solution.py:60
  475.5 7.9 %copy-start.1 = (bf16[96,4096]{1,0:T(8,128)(2,1)S(1)}, bf16[96,4096]{1,0:T(8,128)(2,1)}, u32[]{:S(2)}) copy-start(bf16[96,4096]{1,0:T(8,128)(2,1)} %param.6) | copy-start | bytes 2359300
Sparse Core Ops, SparseCore 0:
  18.4 18.3 all-gather.4
  233.2 48.0 all-gather.6
  283.6 60.4 all-gather.8
